TPU v7x, 512 devices: a whole 4x4x16 slice. The times are simulated.
512 devices in a mesh: seq: 64 (over y, z), slide: 8 (over x, core).
Axes of the slice: x: 4, y: 4, z: 16, core: 2. Of those that a mesh axis runs over, the one named last changes fastest.
Arguments:
- queries: bfloat16 [8, 16384, 1024], P('slide', 'seq'), may hold values from -8 to 8
- key_rows: bfloat16 [8, 16384, 1024], P('slide', 'seq'), may hold values from -8 to 8
- values: bfloat16 [8, 16384, 1024], P('slide', 'seq'), may hold values from -8 to 8
- tissue: int32 [8, 128], P('slide', 'seq'), may hold values 0 or 1
- routes: int32 [8, 1024, 4], P('slide', 'seq'), may hold values from 0 to 63, all different within a row; in each aligned block of 16 rows (0 to 15, 16 to 31, ..., all dimensions but the last counted through in order) at most 2 rows name the same one
Outputs:
- attended: bfloat16 [8, 16384, 1024], P('slide', 'seq')
Inputs may be any that keep to these rules, and one draw needn't show every extreme that they name: `routes`: row t*8 + g belongs to query tile t and pair g; each row names 4 different key blocks; among the rows of one key block (16 rows) no block is named more than 2 times, and some block is named exactly 2 times.
All inputs are finite; a program needn't handle non-finite values. No bound on the sum of `tissue` on one device may be relied on, other than what follows from the above.
Results may differ from a plain program's by a relative error of at most 0.0058.
Values may be sent and summed in bfloat16 or wider, within the bound.
A program may use at most 64 MiB of HBM per device.

v0:
```python
import jax
import jax.numpy as jnp
from jax import lax
from jax.sharding import PartitionSpec as P

TILE = 128
HP = 8


big_negative = -1e30


def slot_ranks(targets, bucket_count):
    onehot = (targets[..., None] == jnp.arange(bucket_count, dtype=jnp.int32)).astype(jnp.int32)
    before = jnp.cumsum(onehot, axis=-2) - onehot
    return jnp.sum(before * onehot, axis=-1)


def block_size(slot_count):
    return max((divisor for divisor in range(1, 17) if slot_count % divisor == 0))


def key_partials(queries_in, pairs_in, own_in, key_pairs, value_pairs, tissue_keys):
    slot_count = queries_in.shape[0]
    tile_rows = queries_in.shape[1]
    head_dim = queries_in.shape[2] // 2
    tokens_here = key_pairs.shape[1]
    block_width = block_size(slot_count)
    block_count = slot_count // block_width
    key_tile = jnp.arange(tokens_here, dtype=jnp.int32) // tile_rows
    score_scale = head_dim ** (-0.5)

    def one_block(block_parts):
        query_block, pair_block, own_block = block_parts
        chosen_keys = key_pairs[pair_block].reshape(block_width, tokens_here, 2, head_dim)
        chosen_values = value_pairs[pair_block].reshape(block_width, tokens_here, 2, head_dim)
        query_four = query_block.reshape(block_width, tile_rows, 2, head_dim)
        scores = (
            jnp.einsum(
                "bqhe,bkhe->bhqk", query_four, chosen_keys, preferred_element_type=jnp.float32
            )
            * score_scale
        )
        usable = tissue_keys[None, :] & (key_tile[None, :] != own_block[:, None])
        key_mask = usable[:, None, None, :]
        scores = jnp.where(key_mask, scores, big_negative)
        shift_max = jnp.max(scores, axis=-1).astype(jnp.bfloat16)
        weights = jnp.where(
            key_mask, jnp.exp(scores - shift_max.astype(jnp.float32)[..., None]), jnp.float32(0.0)
        )
        total_sum = jnp.sum(weights, axis=-1).astype(jnp.bfloat16)
        partial_out = jnp.einsum(
            "bhqk,bkhe->bqhe",
            weights.astype(jnp.bfloat16),
            chosen_values,
            preferred_element_type=jnp.float32,
        )
        return (
            partial_out.astype(jnp.bfloat16).reshape(block_width, tile_rows, 2 * head_dim),
            shift_max,
            total_sum,
        )

    partial_out, shift_max, total_sum = lax.map(
        one_block,
        (
            queries_in.reshape(block_count, block_width, tile_rows, 2 * head_dim),
            pairs_in.reshape(block_count, block_width),
            own_in.reshape(block_count, block_width),
        ),
    )
    return (
        partial_out.reshape(slot_count, tile_rows, 2 * head_dim),
        shift_max.reshape(slot_count, 2, tile_rows),
        total_sum.reshape(slot_count, 2, tile_rows),
    )


def local(queries, key_rows, values, tissue, routes):
    tokens_here = queries.shape[1]
    width_all = queries.shape[2]
    tile_rows = TILE
    tiles_here = tokens_here // tile_rows
    pair_count = HP
    pair_width = width_all // pair_count
    head_dim = pair_width // 2
    unit_count = routes.shape[1]
    span_count = routes.shape[2]
    item_count = unit_count * span_count
    peer_count = lax.axis_size("seq")
    own_index = lax.axis_index("seq")
    capacity = max(2, (2 * item_count + peer_count - 1) // peer_count)
    slot_count = peer_count * capacity
    score_scale = head_dim ** (-0.5)

    def as_units(block_rows):
        return (
            block_rows.reshape(tiles_here, tile_rows, pair_count, pair_width)
            .transpose(0, 2, 1, 3)
            .reshape(unit_count, tile_rows, pair_width)
        )

    query_units = as_units(queries[0])
    own_routes = routes[0]
    targets = own_routes.reshape(item_count)
    ranking = slot_ranks(targets, peer_count)
    slot_of_item = targets * capacity + ranking
    item_unit = jnp.arange(item_count, dtype=jnp.int32) // span_count
    slot_unit = jnp.zeros((slot_count,), jnp.int32).at[slot_of_item].set(item_unit)
    slot_used = jnp.zeros((slot_count,), jnp.bool_).at[slot_of_item].set(True)
    outgoing = jnp.where(
        slot_used[:, None, None], query_units[slot_unit], jnp.zeros((), jnp.bfloat16)
    )
    incoming = lax.all_to_all(
        outgoing.reshape(peer_count, capacity, tile_rows, pair_width),
        "seq",
        split_axis=0,
        concat_axis=0,
        tiled=True,
    )
    incoming = incoming.reshape(slot_count, tile_rows, pair_width)
    every_route = lax.all_gather(own_routes, "seq", axis=0, tiled=True)
    all_targets = every_route.reshape(peer_count, item_count)
    all_ranking = slot_ranks(all_targets, peer_count)
    position = jnp.arange(capacity, dtype=jnp.int32)
    matches = (all_targets[:, None, :] == own_index) & (
        all_ranking[:, None, :] == position[None, :, None]
    )
    unit_here = jnp.sum(matches.astype(jnp.int32) * item_unit[None, None, :], axis=-1).reshape(
        slot_count
    )
    pair_here = unit_here % pair_count
    source = jnp.repeat(jnp.arange(peer_count, dtype=jnp.int32), capacity)
    own_here = jnp.where(source == own_index, unit_here // pair_count, -1)
    key_pairs = key_rows[0].reshape(tokens_here, pair_count, pair_width).transpose(1, 0, 2)
    value_pairs = values[0].reshape(tokens_here, pair_count, pair_width).transpose(1, 0, 2)
    tissue_keys = jnp.repeat(tissue[0] == 1, tile_rows)
    partial_out, shift_max, total_sum = key_partials(
        incoming, pair_here, own_here, key_pairs, value_pairs, tissue_keys
    )
    back_acc, back_shift, back_total = (
        lax.all_to_all(
            partial_out.reshape(peer_count, capacity, tile_rows, pair_width),
            "seq",
            split_axis=0,
            concat_axis=0,
            tiled=True,
        ),
        lax.all_to_all(
            shift_max.reshape(peer_count, capacity, 2, tile_rows),
            "seq",
            split_axis=0,
            concat_axis=0,
            tiled=True,
        ),
        lax.all_to_all(
            total_sum.reshape(peer_count, capacity, 2, tile_rows),
            "seq",
            split_axis=0,
            concat_axis=0,
            tiled=True,
        ),
    )
    listed_acc = back_acc.reshape(slot_count, tile_rows, pair_width)[slot_of_item].reshape(
        unit_count, span_count, tile_rows, 2, head_dim
    )
    listed_shift = (
        back_shift.reshape(slot_count, 2, tile_rows)[slot_of_item]
        .reshape(unit_count, span_count, 2, tile_rows)
        .astype(jnp.float32)
    )
    listed_total = (
        back_total.reshape(slot_count, 2, tile_rows)[slot_of_item]
        .reshape(unit_count, span_count, 2, tile_rows)
        .astype(jnp.float32)
    )
    query_four = query_units.reshape(unit_count, tile_rows, 2, head_dim)
    key_four = as_units(key_rows[0]).reshape(unit_count, tile_rows, 2, head_dim)
    value_four = as_units(values[0]).reshape(unit_count, tile_rows, 2, head_dim)
    own_scores = (
        jnp.einsum("uqhe,ukhe->uhqk", query_four, key_four, preferred_element_type=jnp.float32)
        * score_scale
    )
    own_shift = jnp.max(own_scores, axis=-1)
    own_probs = jnp.exp(own_scores - own_shift[..., None])
    own_total = jnp.sum(own_probs, axis=-1)
    own_partial = jnp.einsum(
        "uhqk,ukhe->uqhe",
        own_probs.astype(jnp.bfloat16),
        value_four,
        preferred_element_type=jnp.float32,
    )
    highest = jnp.maximum(own_shift, jnp.max(listed_shift, axis=1))
    own_weight = jnp.exp(own_shift - highest)
    listed_weight = jnp.exp(listed_shift - highest[:, None])
    numerator = own_partial * own_weight.transpose(0, 2, 1)[..., None] + jnp.sum(
        listed_acc.astype(jnp.float32) * listed_weight.transpose(0, 1, 3, 2)[..., None], axis=1
    )
    denominator = own_weight * own_total + jnp.sum(listed_weight * listed_total, axis=1)
    result = numerator / denominator.transpose(0, 2, 1)[..., None]
    result = result.reshape(tiles_here, pair_count, tile_rows, pair_width).transpose(0, 2, 1, 3)
    return result.reshape(1, tokens_here, width_all).astype(jnp.bfloat16)


def solution(mesh):
    placed = (
        P("slide", "seq", None),
        P("slide", "seq", None),
        P("slide", "seq", None),
        P("slide", "seq"),
        P("slide", "seq", None),
    )
    return jax.shard_map(
        local, mesh=mesh, in_specs=placed, out_specs=P("slide", "seq", None), check_vma=False
    )
```

profile of v0, /device:TPU:6, one launch (start us, length us, event | category | flops | bytes accessed | tf_op | source)
XLA Modules:
  0.0 643.2 jit_solution(16471491676141873427)
XLA Ops:
  2.9 1.1 copy.86
  5.9 3.1 gather_fusion.2
  9.0 4.5 broadcast_select_fusion
  13.5 19.1 %all-to-all-start = ((bf16[64,2,128,128]{3,2,1,0:T(8,128)(2,1)}), bf16[64,2,128,128]{3,2,1,0:T(8,128)(2,1)}, u32[]{:S(2)}, u32[]{:S(2)}) async-start(bf16[64,2,128,128]{3,2,1,0:T(8,128)(2,1)} %broadcast_select_fusion), calls=%async_computation | async-start | bytes 8388608 | tf_op jit(solution)/shard_map/all_to_all | solution.py:114
  32.7 275.6 %all-gather = s32[1,1024,4]{2,0,1:T(1,128)S(1)} all-gather(s32[1,16,4]{2,0,1:T(1,128)S(1)} %copy.71), channel_id=2, replica_groups=mesh['seq'=64,'slide'=8] {'seq'}, dimensions={1}, use_global_device_ids=true | all-gather | bytes 16640 | tf_op jit(solution)/shard_map/all_gather | solution.py:122
  308.9 2.0 reduce.4
  311.2 2.3 fusion.23
  315.0 6.4 copy.79
  321.4 102.2 %while.15 = (s32[]{:T(128)}, bf16[8,16,128,128]{2,3,1,0:T(8,128)(2,1)}, bf16[8,16,2,128]{3,2,1,0:T(2,128)(2,1)S(1)}, bf16[8,16,2,128]{3,2,1,0:T(2,128)(2,1)S(1)}...) while((s32[]{:T(128)}, ...), condition=%wide.region_11.12_spmd.clone, body=%wide.region_8.11_spmd.clone.sunk | while | flops 282336320 | bytes 43122332 | solution.py:64
  322.9 1.1 constant_dynamic-slice_fusion.4
  324.0 1.2 fusion.70
  325.2 2.0 copy-done
  327.2 1.5 fusion.72
  330.0 3.3 fusion.71
  333.3 0.8 constant_dynamic-update-slice_fusion.2
  335.7 1.1 constant_dynamic-slice_fusion.4
  336.8 1.2 fusion.70
  338.0 2.0 copy-done
  339.9 1.5 fusion.72
  342.8 3.3 fusion.71
  346.1 0.9 constant_dynamic-update-slice_fusion.2
  348.4 1.1 constant_dynamic-slice_fusion.4
  349.5 1.2 fusion.70
  350.8 2.0 copy-done
  352.7 1.5 fusion.72
  355.6 3.3 fusion.71
  358.9 0.9 constant_dynamic-update-slice_fusion.2
  361.2 1.1 constant_dynamic-slice_fusion.4
  362.3 1.2 fusion.70
  363.5 2.0 copy-done
  365.5 1.5 fusion.72
  368.3 3.3 fusion.71
  371.7 0.9 constant_dynamic-update-slice_fusion.2
  374.0 1.1 constant_dynamic-slice_fusion.4
  375.1 1.2 fusion.70
  376.3 2.0 copy-done
  378.3 1.5 fusion.72
  381.1 3.3 fusion.71
  384.4 0.9 constant_dynamic-update-slice_fusion.2
  386.8 1.1 constant_dynamic-slice_fusion.4
  387.9 1.2 fusion.70
  389.1 2.0 copy-done
  391.0 1.5 fusion.72
  393.9 3.3 fusion.71
  397.2 0.9 constant_dynamic-update-slice_fusion.2
  399.6 1.1 constant_dynamic-slice_fusion.4
  400.6 1.2 fusion.70
  401.9 2.0 copy-done
  403.8 1.5 fusion.72
  406.7 3.3 fusion.71
  412.3 1.1 constant_dynamic-slice_fusion.4
  413.4 1.2 fusion.70
  414.6 2.0 copy-done
  416.6 1.5 fusion.72
  419.4 3.3 fusion.71
  422.7 0.9 constant_dynamic-update-slice_fusion.2
  423.6 25.4 %all_to_all.20 = bf16[64,2,2,128]{3,2,1,0:T(2,128)(2,1)S(1)} all-to-all(bf16[64,2,2,128]{3,2,1,0:T(2,128)(2,1)S(1)} %bitcast.173), channel_id=1, replica_groups=mesh['seq'=64,'slide'=8] {'seq'}, dimensions={0} | all-to-all | bytes 131072 | tf_op jit(solution)/shard_map/all_to_all | solution.py:149
  449.0 24.1 %all_to_all.21 = bf16[64,2,2,128]{3,2,1,0:T(2,128)(2,1)S(1)} all-to-all(bf16[64,2,2,128]{3,2,1,0:T(2,128)(2,1)S(1)} %bitcast.174), channel_id=1, replica_groups=mesh['seq'=64,'slide'=8] {'seq'}, dimensions={0} | all-to-all | bytes 131072 | tf_op jit(solution)/shard_map/all_to_all | solution.py:156
  473.1 6.1 all-to-all-start.2
  480.4 1.1 copy.69
  483.9 150.6 %all-to-all-done.2 = bf16[64,2,128,128]{2,3,1,0:T(8,128)(2,1)} async-done(((bf16[64,2,128,128]{2,3,1,0:T(8,128)(2,1)}), bf16[64,2,128,128]{2,3,1,0:T(8,128)(2,1)}, u32[]{:S(2)}, u32[]{:S(2)}) %all-to-all-start.2) | async-done | bytes 4194336 | tf_op jit(solution)/shard_map/all_to_all | solution.py:142
  634.5 4.3 gather_fusion.4
  638.9 2.3 fusion.19
  642.2 1.0 convert_element_type.102
  (179 shorter events, 34.7 us)
Async XLA Ops:
  4.1 0.8 copy-start.1
  13.5 19.1 %copy-start.8 = (s32[1,16,4]{1,2,0:T(4,128)S(1)}, s32[1,16,4]{1,2,0:T(4,128)}, u32[]{:S(2)}) copy-start(s32[1,16,4]{1,2,0:T(4,128)} %param.11) | copy-start | bytes 772
  13.5 300.5 %copy-start.5 = (bf16[1,256,1024]{2,1,0:T(8,128)(2,1)S(1)}, bf16[1,256,1024]{2,1,0:T(8,128)(2,1)}, u32[]{:S(2)}) copy-start(bf16[1,256,1024]{2,1,0:T(8,128)(2,1)} %param.9) | copy-start | bytes 1572868
  13.5 301.5 %all-to-all-start = ((bf16[64,2,128,128]{3,2,1,0:T(8,128)(2,1)}), bf16[64,2,128,128]{3,2,1,0:T(8,128)(2,1)}, u32[]{:S(2)}, u32[]{:S(2)}) async-start(bf16[64,2,128,128]{3,2,1,0:T(8,128)(2,1)} %broadcast_select_fusion), calls=%async_computation | async-start | bytes 8388608 | tf_op jit(solution)/shard_map/all_to_all | solution.py:114
  32.6 281.9 %copy-start.3 = (bf16[1,256,1024]{2,1,0:T(8,128)(2,1)S(1)}, bf16[1,256,1024]{2,1,0:T(8,128)(2,1)}, u32[]{:S(2)}) copy-start(bf16[1,256,1024]{2,1,0:T(8,128)(2,1)} %param.8) | copy-start | bytes 1572868
  32.6 282.3 %copy-start.9 = (s32[1,2]{1,0:T(1,128)S(1)}, s32[1,2]{1,0:T(1,128)}, u32[]{:S(2)}) copy-start(s32[1,2]{1,0:T(1,128)} %param.10) | copy-start | bytes 28
  325.2 2.0 copy-start
  337.9 2.0 copy-start
  350.7 2.0 copy-start
  363.5 2.0 copy-start
  376.3 2.0 copy-start
  389.1 2.0 copy-start
  401.8 2.0 copy-start
  414.6 2.0 copy-start
  473.1 6.1 copy-start.2
  473.1 6.5 %copy-start.4 = (bf16[1,256,1024]{2,1,0:T(8,128)(2,1)S(1)}, bf16[1,256,1024]{2,1,0:T(8,128)(2,1)}, u32[]{:S(2)}) copy-start(bf16[1,256,1024]{2,1,0:T(8,128)(2,1)} %param.8) | copy-start | bytes 1572868
  473.1 161.4 %all-to-all-start.2 = ((bf16[64,2,128,128]{2,3,1,0:T(8,128)(2,1)}), bf16[64,2,128,128]{2,3,1,0:T(8,128)(2,1)}, u32[]{:S(2)}, u32[]{:S(2)}) async-start(bf16[64,2,128,128]{2,3,1,0:T(8,128)(2,1)} %bitcast.22), calls=%async_computation.2 | async-start | bytes 8388608 | tf_op jit(solution)/shard_map/all_to_all | solution.py:142
  479.2 1.0 copy-start.6
  482.4 158.8 %copy-start.7 = (bf16[2,8,128,128]{2,3,1,0:T(8,128)(2,1)S(1)}, bf16[2,8,128,128]{2,3,1,0:T(8,128)(2,1)}, u32[]{:S(2)}) copy-start(bf16[2,8,128,128]{2,3,1,0:T(8,128)(2,1)} %copy.69) | copy-start | bytes 1572868
where the time goes:
time: 645 us; the launch traced here: 643 us
  blocking collectives  325 us (50%)
  waiting for transfers between devices  151 us (23%)
  local copies, waits for them, and re-layouts  78.3 us (12%)
  matrix products  37.2 us (6%)
  other arithmetic  25.8 us (4%)
  starting transfers between devices  25.2 us (4%)
    all_gather x1, blocking collectives, local(): every_route = lax.all_gather(own_routes, 'seq', axis=0, tiled=True)  276 us
    all_to_all x1, waiting for transfers between devices, local(): lax.all_to_all(partial_out.reshape(peer_count, capacity, tile_rows, pair_...  151 us
    dot_general x8, matrix products, one_block(): jnp.einsum('bhqk,bkhe->bqhe', weights.astype(jnp.bfloat16), chosen_values...  26.5 us
    all_to_all x1, blocking collectives, local(): lax.all_to_all(shift_max.reshape(peer_count, capacity, 2, tile_rows), 'se...  25.4 us
    all_to_all x1, blocking collectives, local(): lax.all_to_all(total_sum.reshape(peer_count, capacity, 2, tile_rows), 'se...  24.1 us
    all_to_all x1, starting transfers between devices, local(): lax.all_to_all(outgoing.reshape(peer_count, capacity, tile_rows, pair_wid...  19.1 us
    while x16, local copies, waits for them, and re-layouts  15.6 us
  transfers between devices with their start and end apart: 2, of which 1 were waited for; matrix products, arithmetic and copies ran while one was open for 2% of the time, Pallas kernels for 0%

commit v1 on v0

v1 whole, which is shorter than its diff:
```python
import jax
import jax.numpy as jnp
from jax import lax
from jax.experimental import pallas as pl
from jax.experimental.pallas import tpu as pltpu
from jax.sharding import PartitionSpec as P

NY = 4
NZ = 16
TILE = 128
HP = 8
PAIR = 128
HALF = NZ // 2
WINDOW = HP // 2
UNITS = 16
SPAN = 4
ROWS = 144

big_negative = -1e30
MESH = pl.DeviceIdType.MESH


def halves(unit):
    mid = PAIR // 2
    zero = jnp.zeros((mid, TILE), unit.dtype)
    upper = jnp.concatenate([unit[:mid], zero], axis=1)
    return jnp.concatenate([upper, jnp.concatenate([zero, unit[mid:]], axis=1)], axis=0)


def fold(both):
    mid = PAIR // 2
    return jnp.concatenate([both[:mid, :TILE], both[mid:, TILE:]], axis=0)


def by_head(pair_row):
    return pair_row[:, :TILE], pair_row[:, TILE:]


def kernel(
    tissue_hbm, routes_hbm, q_hbm, k_hbm, v_hbm, out,
    tissue, routes, q_rows, k_rows, v_rows, kv, tis, work_o, work_r, work_l, qs, tab, tabv, tabs, tabo, places,
    ret_out, ret_in, own_acc, own_stat,
    rs, rr, ls, lr, trs, trr, tls, tlr, q_send, q_recv, t_send, t_recv, ret_s, ret_r, loc,
):
    me = lax.axis_index("seq")
    y, z = me // NZ, me % NZ

    loads = [
        pltpu.make_async_copy(k_hbm.at[0], k_rows, loc.at[0]),
        pltpu.make_async_copy(v_hbm.at[0], v_rows, loc.at[1]),
        pltpu.make_async_copy(q_hbm.at[0], q_rows, loc.at[2]),
        pltpu.make_async_copy(routes_hbm.at[0], routes, loc.at[5]),
        pltpu.make_async_copy(tissue_hbm, tissue, loc.at[6]),
    ]
    for load in loads:
        load.start()

    def at(row, column):
        return {"seq": row % NY * NZ + column % NZ}

    right, left = at(y, z + 1), at(y, z + NZ - 1)

    def peer(dy):
        return at(y + dy, z)

    def remote(src, dst, send, recv, device):
        return pltpu.make_async_remote_copy(
            src_ref=src, dst_ref=dst, send_sem=send, recv_sem=recv,
            device_id=device, device_id_type=MESH,
        )

    barrier = pltpu.get_barrier_semaphore()
    for device in [right, left] + [peer(dy) for dy in range(1, NY)]:
        pl.semaphore_signal(barrier, inc=1, device_id=device, device_id_type=MESH)

    def chunk_right(s, c):
        return remote(kv.at[s - 1, c], kv.at[s, c], rs.at[s, c], rr.at[s, c], right)

    def chunk_left(s, c):
        pair = (c + WINDOW) % HP
        return remote(
            kv.at[(NZ + 1 - s) % NZ, pair], kv.at[NZ - s, pair], ls.at[s, c], lr.at[s, c], left
        )

    def tis_right(s):
        return remote(tis.at[s - 1], tis.at[s], trs.at[s], trr.at[s], right)

    def tis_left(s):
        return remote(tis.at[(NZ + 1 - s) % NZ], tis.at[NZ - s], tls.at[s], tlr.at[s], left)

    def tab_copy(dy):
        back = (NY - dy) % NY
        return remote(tab.at[dy], tabv.at[back], t_send.at[dy], t_recv.at[back], peer(dy))

    half = UNITS // 2

    def q_up(part):
        units = pl.ds(part * half, half)
        return remote(qs.at[0, units], qs.at[NY - 1, units], q_send.at[0, part], q_recv.at[0, part], peer(1))

    def q_down(part):
        units = pl.ds(part * half, half)
        return remote(qs.at[0, units], qs.at[1, units], q_send.at[1, part], q_recv.at[1, part], peer(NY - 1))

    def q_on_up():
        units = pl.ds(0, half)
        return remote(qs.at[NY - 1, units], qs.at[2, units], q_send.at[2, 0], q_recv.at[2, 0], peer(1))

    def q_on_down():
        units = pl.ds(half, half)
        return remote(qs.at[1, units], qs.at[2, units], q_send.at[2, 1], q_recv.at[2, 1], peer(NY - 1))

    def lay_pair(g):
        columns = slice(g * PAIR, (g + 1) * PAIR)
        for t in range(2):
            tokens = slice(t * TILE, (t + 1) * TILE)
            kv[0, g, t] = k_rows[tokens, columns]
            kv[0, g, 2 + t] = v_rows[tokens, columns].T

    loads[0].wait()
    loads[1].wait()
    for c in range(WINDOW):
        lay_pair(c)
        lay_pair(c + WINDOW)
        if c == 0:
            pl.semaphore_wait(barrier, 2 + NY - 1)
        chunk_right(1, c).start()
        chunk_left(1, c).start()

    for load in loads[3:]:
        load.wait()
    for t in range(2):
        tis[0, t] = jnp.full((8, 128), (tissue[0, t] == 1).astype(jnp.int32), jnp.int32)
    tis_right(1).start()
    tis_left(1).start()

    lane = lax.broadcasted_iota(jnp.int32, (8, 128), 1)
    row = lax.broadcasted_iota(jnp.int32, (8, 128), 0)
    block = (y + row) % NY * NZ + (z + NZ - (lane // 2) % NZ) % NZ
    first = jnp.full((8, 128), UNITS - 1, jnp.int32)
    last = jnp.zeros((8, 128), jnp.int32)
    for u in range(UNITS):
        named = block == routes[0, u]
        for j in range(1, SPAN):
            named = named | (block == routes[j, u])
        first = jnp.where(named, jnp.minimum(first, u), first)
        last = jnp.where(named, u, last)
    table = jnp.where(lane % 2 == 0, first, last)
    for dy in range(NY):
        tab[dy] = jnp.broadcast_to(table[dy : dy + 1], (8, 128))
    for dy in range(1, NY):
        tab_copy(dy).start()

    scale = jnp.bfloat16((PAIR // 2) ** -0.5)
    loads[2].wait()

    def lay_queries(part):
        for i in range(half):
            u = part * half + i
            tile, g = u // HP, u % HP
            qs[0, u] = (q_rows[tile * TILE : (tile + 1) * TILE, g * PAIR : (g + 1) * PAIR] * scale).T

    lay_queries(0)
    q_up(0).start()
    lay_queries(1)
    q_down(1).start()
    q_up(1).start()
    q_down(0).start()

    def own_units(low, count):
        numbers = [low + i for i in range(count)]

        def scores_of(u):
            return jnp.dot(
                kv[0, u % HP, u // HP], halves(qs[0, u]), preferred_element_type=jnp.float32
            )

        scores = scores_of(numbers[0])
        done = []
        for i, u in enumerate(numbers):
            later = scores_of(numbers[i + 1]) if i + 1 < count else None
            shift = jnp.max(scores, axis=0, keepdims=True)
            probs = jnp.exp(scores - shift)
            total = jnp.sum(probs, axis=0, keepdims=True)
            both = jnp.dot(
                kv[0, u % HP, 2 + u // HP], probs.astype(jnp.bfloat16), preferred_element_type=jnp.float32
            )
            done.append((u, fold(both), by_head(shift) + by_head(total)))
            scores = later
        for u, folded, four in done:
            own_acc[u] = folded
            own_stat[u] = jnp.concatenate(four + four, axis=0)

    def slots(jobs):
        def scores_of(job):
            work, d, dy, c = job
            u = tabs[dy, 0, d * 2 + c]
            g = u & (HP - 1)
            unit = halves(qs[dy, u])
            keep = []
            for t in range(2):
                row = tis[d, t, 0:1, :]
                if work is work_o:
                    row = row * (1 - ((dy == 0) & ((u >> 3) == t)).astype(jnp.int32))
                keep.append(jnp.concatenate([row, row], axis=1) != 0)
            value = jnp.concatenate([work[g, 2], work[g, 3]], axis=1)
            keys = jnp.concatenate([work[g, 0], work[g, 1]], axis=0)
            both = jnp.dot(keys, unit, preferred_element_type=jnp.float32)
            return [both[:TILE], both[TILE:]], keep, value

        ready = scores_of(jobs[0])
        done = []
        for i, job in enumerate(jobs):
            later = scores_of(jobs[i + 1]) if i + 1 < len(jobs) else None
            scores, keep, value = ready
            peaks = [
                jnp.where(keep[t], jnp.max(scores[t], axis=0, keepdims=True), big_negative)
                for t in range(2)
            ]
            shift = jnp.maximum(peaks[0], peaks[1]).astype(jnp.bfloat16).astype(jnp.float32)
            weights = [
                jnp.exp(scores[t] - jnp.where(keep[t], shift, -big_negative)) for t in range(2)
            ]
            total = jnp.sum(weights[0], axis=0, keepdims=True) + jnp.sum(weights[1], axis=0, keepdims=True)
            both = jnp.dot(
                value,
                jnp.concatenate([w.astype(jnp.bfloat16) for w in weights], axis=0),
                preferred_element_type=jnp.float32,
            )
            four = by_head(shift) + by_head(total)
            done.append((job, fold(both), jnp.concatenate(four * 4, axis=0)))
            ready = later
        for (work, d, dy, c), folded, stat in done:
            ret_out[dy, d, c, 0:PAIR, :] = folded.astype(jnp.bfloat16)
            ret_out[dy, d, c, PAIR:ROWS, :] = stat.astype(jnp.bfloat16)

    def ret_copy(dy, d):
        back = (NY - dy) % NY
        return remote(
            ret_out.at[dy, d], ret_in.at[back * NZ + d], ret_s.at[dy, d], ret_r.at[back, d], peer(dy)
        )

    def ret_local(d):
        return pltpu.make_async_copy(ret_out.at[0, d], ret_in.at[d], ret_r.at[0, d])

    def give_back(dy, d):
        @pl.when(dy == 0)
        def _():
            ret_local(d).start()

        @pl.when(dy > 0)
        def _():
            ret_copy(dy, d).start()

    def ret_wait(d):
        ret_local(d).wait()
        for dy in range(1, NY):
            ret_copy(dy, d).wait_send()
            ret_copy(dy, d).wait_recv()

    def fill(work, d):
        for g in range(HP):
            work[g] = kv[d, g]

    def relay(s, c):
        later, chunk = s + (c + WINDOW) // HP, (c + WINDOW) % HP
        chunk_right(s, c).wait_send()
        chunk_right(later, chunk).start()
        chunk_left(s, c).wait_send()
        chunk_left(later, chunk).start()
        chunk_right(s, c).wait_recv()
        chunk_left(s, c).wait_recv()

    def relay_tissue(s):
        tis_right(s).wait_recv()
        tis_right(s + 1).start()
        tis_left(s).wait_recv()

        @pl.when(s < HALF - 1)
        def _():
            tis_left(s + 1).start()

        tis_right(s).wait_send()
        tis_left(s).wait_send()

    relay_tissue(1)

    def first_points(low, high):
        @pl.loop(low, high)
        def _(c):
            relay(1, c)
            own_units(2 * c, 2)

    first_points(0, HP - 3)
    q_up(0).wait_recv()
    q_on_up().start()
    q_down(1).wait_recv()
    q_on_down().start()
    first_points(HP - 3, HP)

    for dy in range(1, NY):
        tab_copy(dy).wait_recv()
    tabv[0] = tab[0]
    moves = [pltpu.make_async_copy(tabv, tabs, loc.at[3]), pltpu.make_async_copy(tab, tabo, loc.at[4])]
    for move in moves:
        move.start()
    for move in moves:
        move.wait()
    q_up(1).wait_recv()
    q_down(0).wait_recv()
    q_on_up().wait_recv()
    q_on_down().wait_recv()
    fill(work_o, 0)

    def find_places():
        @pl.loop(0, UNITS)
        def _(u):
            for j in range(SPAN):
                b = routes[j, u]
                dy = ((b >> 4) + NY - y) & (NY - 1)
                d = (z + NZ - (b & (NZ - 1))) & (NZ - 1)
                places[2 * (u * SPAN + j)] = dy * NZ + d
                places[2 * (u * SPAN + j) + 1] = (tabo[dy, 0, 2 * d] != u).astype(jnp.int32)

    @pl.loop(2, HALF + 1)
    def _(s):
        before_r, before_l = s - 1, NZ + 1 - s

        @pl.when(s < HALF)
        def _():
            relay_tissue(s)

        fill(work_r, before_r)
        fill(work_l, before_l)

        @pl.when(s == 3)
        def _():
            find_places()
            for dy in range(1, NY):
                tab_copy(dy).wait_send()
            for part in range(2):
                q_up(part).wait_send()
                q_down(part).wait_send()
            q_on_up().wait_send()
            q_on_down().wait_send()

        @pl.when(s == 4)
        def _():
            ret_wait(0)

        @pl.when(s >= 4)
        def _():
            ret_wait(s - 3)
            ret_wait(NZ + 3 - s)

        @pl.loop(0, NY)
        def _(dy):
            @pl.when(s < HALF)
            def _():
                relay(s, 2 * dy)
                relay(s, 2 * dy + 1)

            slots([(work, d, dy, c) for work, d in ((work_r, before_r), (work_l, before_l)) for c in range(2)])
            give_back(dy, before_r)
            give_back(dy, before_l)

            @pl.when(s == 2)
            def _():
                slots([(work_o, 0, dy, c) for c in range(2)])
                give_back(dy, 0)

    tis_right(HALF).wait_send()
    tis_right(HALF).wait_recv()
    for d in (HALF - 2, HALF + 2, HALF - 1, HALF + 1):
        ret_wait(d)

    for c in range(WINDOW):
        chunk_right(HALF, c).wait_recv()
        work_r[c] = kv[HALF, c]
        chunk_left(HALF, c).wait_recv()
        work_r[c + WINDOW] = kv[HALF, c + WINDOW]

    @pl.loop(0, NY // 2)
    def _(i):
        pair = [2 + i, 1 - i]
        slots([(work_r, HALF, dy, c) for dy in pair for c in range(2)])
        for dy in pair:
            give_back(dy, HALF)

    for c in range(WINDOW):
        chunk_right(HALF, c).wait_send()
        chunk_left(HALF, c).wait_send()
    ret_wait(HALF)

    mid = PAIR // 2

    def combine(u):
        tile, g = u // HP, u % HP
        spots = [(places[2 * (u * SPAN + j)], places[2 * (u * SPAN + j) + 1]) for j in range(SPAN)]
        stats = [ret_in[a, c, PAIR:ROWS, :].astype(jnp.float32) for a, c in spots]
        own = own_stat[u]
        rows = []
        for h in range(2):
            span = slice(h * mid, (h + 1) * mid)
            shifts = [st[h : h + 1, :] for st in stats]
            totals = [st[2 + h : 3 + h, :] for st in stats]
            top = own[h : h + 1, :]
            for sh in shifts:
                top = jnp.maximum(top, sh)
            own_w = jnp.exp(own[h : h + 1, :] - top)
            ws = [jnp.exp(sh - top) for sh in shifts]
            den = own_w * own[2 + h : 3 + h, :]
            for w, t in zip(ws, totals):
                den = den + w * t
            inv = 1.0 / den
            num = own_acc[u, span, :] * (own_w * inv)
            for (a, c), w in zip(spots, ws):
                num = num + ret_in[a, c, span, :].astype(jnp.float32) * (w * inv)
            rows.append(num)
        result = jnp.concatenate(rows, axis=0)
        rows_at = pl.ds(pl.multiple_of(tile * TILE, TILE), TILE)
        out[rows_at, pl.ds(pl.multiple_of(g * PAIR, PAIR), PAIR)] = result.T.astype(jnp.bfloat16)

    @pl.loop(0, UNITS // 4)
    def _(i):
        for k in range(4):
            combine(4 * i + k)


def local(queries, key_rows, values, tissue, routes):
    vmem = pl.BlockSpec(memory_space=pltpu.VMEM)
    hbm = pl.BlockSpec(memory_space=pltpu.HBM)
    dma = pltpu.SemaphoreType.DMA
    steps = HALF + 1
    rows = (2 * TILE, HP * PAIR)
    block = (HP, 4, PAIR, TILE)
    out = pl.pallas_call(
        kernel,
        out_shape=jax.ShapeDtypeStruct(rows, jnp.bfloat16),
        in_specs=[hbm] * 5,
        out_specs=vmem,
        scratch_shapes=[
            pltpu.SMEM((1, 2), jnp.int32),
            pltpu.SMEM((SPAN, UNITS), jnp.int32),
            pltpu.VMEM(rows, jnp.bfloat16),
            pltpu.VMEM(rows, jnp.bfloat16),
            pltpu.VMEM(rows, jnp.bfloat16),
            pltpu.VMEM((NZ,) + block, jnp.bfloat16),
            pltpu.VMEM((NZ, 2, 8, 128), jnp.int32),
            pltpu.VMEM(block, jnp.bfloat16),
            pltpu.VMEM(block, jnp.bfloat16),
            pltpu.VMEM(block, jnp.bfloat16),
            pltpu.VMEM((NY, UNITS, PAIR, TILE), jnp.bfloat16),
            pltpu.VMEM((NY, 8, 128), jnp.int32),
            pltpu.VMEM((NY, 8, 128), jnp.int32),
            pltpu.SMEM((NY, 8, 128), jnp.int32),
            pltpu.SMEM((NY, 8, 128), jnp.int32),
            pltpu.SMEM((2 * UNITS * SPAN,), jnp.int32),
            pltpu.VMEM((NY, NZ, 2, ROWS, TILE), jnp.bfloat16),
            pltpu.VMEM((NY * NZ, 2, ROWS, TILE), jnp.bfloat16),
            pltpu.VMEM((UNITS, PAIR, TILE), jnp.float32),
            pltpu.VMEM((UNITS, 8, 128), jnp.float32),
            dma((steps, HP)), dma((steps, HP)), dma((steps, HP)), dma((steps, HP)),
            dma((steps,)), dma((steps,)), dma((steps,)), dma((steps,)),
            dma((3, 2)), dma((3, 2)), dma((NY,)), dma((NY,)),
            dma((NY, NZ)), dma((NY, NZ)), dma((7,)),
        ],
        compiler_params=pltpu.CompilerParams(
            collective_id=0, has_side_effects=True, vmem_limit_bytes=53 * 1024 * 1024
        ),
    )(tissue, routes.transpose(0, 2, 1), queries, key_rows, values)
    return out[None]


def solution(mesh):
    placed = (
        P("slide", "seq", None),
        P("slide", "seq", None),
        P("slide", "seq", None),
        P("slide", "seq"),
        P("slide", "seq", None),
    )
    return jax.shard_map(
        local, mesh=mesh, in_specs=placed, out_specs=P("slide", "seq", None), check_vma=False
    )
```

time: 645 us -> 199 us (0.31)
  blocking collectives: 325 us -> 0 us
  Pallas kernels: 0 us -> 197 us
  waiting for transfers between devices: 151 us -> 0 us
  local copies, waits for them, and re-layouts: 78.3 us -> 2.13 us
  matrix products: 37.2 us -> 0 us
  other arithmetic: 25.8 us -> 0 us
  starting transfers between devices: 25.2 us -> 0 us
    all_gather x1 -> x0, blocking collectives: 276 us -> none  [local(): every_route = lax.all_gather(own_routes, 'seq', axis=0, tiled=True)]
    pallas_call x0 -> x1, Pallas kernels: none -> 197 us  [local(): pl.pallas_call(kernel, out_shape=jax.ShapeDtypeStruct(rows, jnp.bfloat16)...]
    all_to_all x2 -> x0, waiting for transfers between devices: 151 us -> none  [the longest x1 151 us: local(): lax.all_to_all(partial_out.reshape(peer_count, capacity, tile_rows, pair_...]
    all_to_all x2 -> x0, blocking collectives: 49.5 us -> none  [the longest x1 25.4 us: local(): lax.all_to_all(shift_max.reshape(peer_count, capacity, 2, tile_rows), 'se...]
    dot_general x18 -> x0, matrix products: 37.2 us -> none  [the longest x8 26.5 us: one_block(): jnp.einsum('bhqk,bkhe->bqhe', weights.astype(jnp.bfloat16), chosen_values...]
    gather x36 -> x0, local copies, waits for them, and re-layouts: 29.2 us -> none  [the longest x16 10.2 us: one_block(): value_pairs[pair_block].reshape(block_width, tokens_here, 2, head_dim)]
    all_to_all x2 -> x0, starting transfers between devices: 25.2 us -> none  [the longest x1 19.1 us: local(): lax.all_to_all(outgoing.reshape(peer_count, capacity, tile_rows, pair_wid...]
    while x16 -> x0, local copies, waits for them, and re-layouts: 15.6 us -> none
  transfers between devices with their start and end apart: 2 -> 0, of which waited for: 1 -> 0; matrix products, arithmetic and copies ran while one was open for 2% -> 0% of each run, Pallas kernels for 0% -> 0%
where the time goes in v1:
time: 199 us
  Pallas kernels  197 us (99%)
  local copies, waits for them, and re-layouts  2.13 us (1%)
    pallas_call x1, Pallas kernels, local(): pl.pallas_call(kernel, out_shape=jax.ShapeDtypeStruct(rows, jnp.bfloat16)...  197 us

profile of v1, /device:TPU:6, one launch (start us, length us, event | category | flops | bytes accessed | tf_op | source)
XLA Modules:
  0.0 198.9 jit_solution(379000949383867088)
XLA Ops:
  0.0 0.0 copy-start.1
  0.0 0.7 copy-done.1
  0.7 0.0 copy-start
  0.7 0.7 copy-done
  1.3 196.7 %shard_map.55 = bf16[256,1024]{1,0:T(8,128)(2,1)S(1)} custom-call(s32[1,2]{1,0:T(1,128)S(1)} %copy-done.1, s32[1,4,16]{2,1,0:T(4,128)S(1)} %bitcast.3, bf16[1,256,1024]{2,1,0:T(8,128)(2,1)} %q_hbm.1, bf16[1,256,1024]{2,1,0:T(8,128)(2,1)} %k_hbm.1, bf16[1,256,1024]{2,1,0:T(8,128)(2,1)} %v_hbm.1), custom_call_target="tpu_custom_call" | custom-call | tf_op jit(solution)/shard_map/pallas_call | solution.py:437
  198.1 0.8 copy.7
Async XLA Ops:
  0.0 0.7 copy-start.1
  0.7 0.7 copy-start

commit v2 on v1

--- a/solution.py
+++ b/solution.py
@@ -14,7 +14,8 @@
 WINDOW = HP // 2
 UNITS = 16
 SPAN = 4
-ROWS = 144
+PIECE = 16
+PIECES = PAIR // PIECE
 
 big_negative = -1e30
 MESH = pl.DeviceIdType.MESH
@@ -82,6 +83,20 @@
             kv.at[(NZ + 1 - s) % NZ, pair], kv.at[NZ - s, pair], ls.at[s, c], lr.at[s, c], left
         )
 
+    def first_hop(c, pair, slot_at, send, recv, device):
+        columns = pl.ds(pl.multiple_of(pair * PAIR, PAIR), PAIR)
+        for i, src in enumerate((k_hbm, v_hbm)):
+            for t in range(2):
+                tokens = pl.ds(t * TILE, TILE)
+                remote(
+                    src.at[0, tokens, columns], kv.at[slot_at, pair, 2 * i + t],
+                    send.at[1, c], recv.at[1, c], device,
+                ).start()
+
+    def start_first(c):
+        first_hop(c, c, 1, rs, rr, right)
+        first_hop(c, (c + WINDOW) % HP, NZ - 1, ls, lr, left)
+
     def tis_right(s):
         return remote(tis.at[s - 1], tis.at[s], trs.at[s], trr.at[s], right)
 
@@ -114,18 +129,12 @@
         columns = slice(g * PAIR, (g + 1) * PAIR)
         for t in range(2):
             tokens = slice(t * TILE, (t + 1) * TILE)
-            kv[0, g, t] = k_rows[tokens, columns]
-            kv[0, g, 2 + t] = v_rows[tokens, columns].T
-
-    loads[0].wait()
-    loads[1].wait()
+            work_o[g, t] = k_rows[tokens, columns]
+            work_o[g, 2 + t] = v_rows[tokens, columns].T
+
+    pl.semaphore_wait(barrier, 2 + NY - 1)
     for c in range(WINDOW):
-        lay_pair(c)
-        lay_pair(c + WINDOW)
-        if c == 0:
-            pl.semaphore_wait(barrier, 2 + NY - 1)
-        chunk_right(1, c).start()
-        chunk_left(1, c).start()
+        start_first(c)
 
     for load in loads[3:]:
         load.wait()
@@ -167,12 +176,17 @@
     q_up(1).start()
     q_down(0).start()
 
+    loads[0].wait()
+    loads[1].wait()
+    for g in range(HP):
+        lay_pair(g)
+
     def own_units(low, count):
         numbers = [low + i for i in range(count)]
 
         def scores_of(u):
             return jnp.dot(
-                kv[0, u % HP, u // HP], halves(qs[0, u]), preferred_element_type=jnp.float32
+                work_o[u % HP, u // HP], halves(qs[0, u]), preferred_element_type=jnp.float32
             )
 
         scores = scores_of(numbers[0])
@@ -183,7 +197,7 @@
             probs = jnp.exp(scores - shift)
             total = jnp.sum(probs, axis=0, keepdims=True)
             both = jnp.dot(
-                kv[0, u % HP, 2 + u // HP], probs.astype(jnp.bfloat16), preferred_element_type=jnp.float32
+                work_o[u % HP, 2 + u // HP], probs.astype(jnp.bfloat16), preferred_element_type=jnp.float32
             )
             done.append((u, fold(both), by_head(shift) + by_head(total)))
             scores = later
@@ -228,11 +242,14 @@
                 preferred_element_type=jnp.float32,
             )
             four = by_head(shift) + by_head(total)
-            done.append((job, fold(both), jnp.concatenate(four * 4, axis=0)))
+            done.append((job, fold(both), jnp.concatenate(four * 2, axis=0)))
             ready = later
-        for (work, d, dy, c), folded, stat in done:
-            ret_out[dy, d, c, 0:PAIR, :] = folded.astype(jnp.bfloat16)
-            ret_out[dy, d, c, PAIR:ROWS, :] = stat.astype(jnp.bfloat16)
+        for i, ((work, d, dy, c), folded, stat) in enumerate(done):
+            pieces = folded.astype(jnp.bfloat16).reshape(PIECES, PIECE, TILE)
+            ret_out[dy, d, c * PIECES : (c + 1) * PIECES] = pieces
+            if c == 1:
+                both = jnp.concatenate([done[i - 1][2], stat], axis=0)
+                ret_out[dy, d, 2 * PIECES] = both.astype(jnp.bfloat16)
 
     def ret_copy(dy, d):
         back = (NY - dy) % NY
@@ -258,16 +275,29 @@
             ret_copy(dy, d).wait_send()
             ret_copy(dy, d).wait_recv()
 
+    def fill_pair(work, d, g):
+        for t in range(2):
+            work[g, t] = kv[d, g, t]
+            work[g, 2 + t] = kv[d, g, 2 + t].T
+
     def fill(work, d):
         for g in range(HP):
-            work[g] = kv[d, g]
+            fill_pair(work, d, g)
 
     def relay(s, c):
         later, chunk = s + (c + WINDOW) // HP, (c + WINDOW) % HP
         chunk_right(s, c).wait_send()
-        chunk_right(later, chunk).start()
         chunk_left(s, c).wait_send()
-        chunk_left(later, chunk).start()
+
+        @pl.when(later == 1)
+        def _():
+            start_first(chunk)
+
+        @pl.when(later > 1)
+        def _():
+            chunk_right(later, chunk).start()
+            chunk_left(later, chunk).start()
+
         chunk_right(s, c).wait_recv()
         chunk_left(s, c).wait_recv()
 
@@ -310,7 +340,6 @@
     q_down(0).wait_recv()
     q_on_up().wait_recv()
     q_on_down().wait_recv()
-    fill(work_o, 0)
 
     def find_places():
         @pl.loop(0, UNITS)
@@ -376,9 +405,9 @@
 
     for c in range(WINDOW):
         chunk_right(HALF, c).wait_recv()
-        work_r[c] = kv[HALF, c]
+        fill_pair(work_r, HALF, c)
         chunk_left(HALF, c).wait_recv()
-        work_r[c + WINDOW] = kv[HALF, c + WINDOW]
+        fill_pair(work_r, HALF, c + WINDOW)
 
     @pl.loop(0, NY // 2)
     def _(i):
@@ -397,7 +426,10 @@
     def combine(u):
         tile, g = u // HP, u % HP
         spots = [(places[2 * (u * SPAN + j)], places[2 * (u * SPAN + j) + 1]) for j in range(SPAN)]
-        stats = [ret_in[a, c, PAIR:ROWS, :].astype(jnp.float32) for a, c in spots]
+        stats = []
+        for a, c in spots:
+            both = ret_in[a, 2 * PIECES].astype(jnp.float32)
+            stats.append(jnp.where(c == 0, both[0:8], both[8:16]))
         own = own_stat[u]
         rows = []
         for h in range(2):
@@ -415,7 +447,9 @@
             inv = 1.0 / den
             num = own_acc[u, span, :] * (own_w * inv)
             for (a, c), w in zip(spots, ws):
-                num = num + ret_in[a, c, span, :].astype(jnp.float32) * (w * inv)
+                first = c * PIECES + h * (PIECES // 2)
+                part = jnp.concatenate([ret_in[a, first + i] for i in range(PIECES // 2)], axis=0)
+                num = num + part.astype(jnp.float32) * (w * inv)
             rows.append(num)
         result = jnp.concatenate(rows, axis=0)
         rows_at = pl.ds(pl.multiple_of(tile * TILE, TILE), TILE)
@@ -456,8 +490,8 @@
             pltpu.SMEM((NY, 8, 128), jnp.int32),
             pltpu.SMEM((NY, 8, 128), jnp.int32),
             pltpu.SMEM((2 * UNITS * SPAN,), jnp.int32),
-            pltpu.VMEM((NY, NZ, 2, ROWS, TILE), jnp.bfloat16),
-            pltpu.VMEM((NY * NZ, 2, ROWS, TILE), jnp.bfloat16),
+            pltpu.VMEM((NY, NZ, 2 * PIECES + 1, PIECE, TILE), jnp.bfloat16),
+            pltpu.VMEM((NY * NZ, 2 * PIECES + 1, PIECE, TILE), jnp.bfloat16),
             pltpu.VMEM((UNITS, PAIR, TILE), jnp.float32),
             pltpu.VMEM((UNITS, 8, 128), jnp.float32),
             dma((steps, HP)), dma((steps, HP)), dma((steps, HP)), dma((steps, HP)),

time: 199 us -> 200 us (level)
  no operation moved by 1% of the time
where the time goes in v2:
time: 200 us
  Pallas kernels  198 us (99%)
  local copies, waits for them, and re-layouts  2.13 us (1%)
    pallas_call x1, Pallas kernels, local(): pl.pallas_call(kernel, out_shape=jax.ShapeDtypeStruct(rows, jnp.bfloat16)...  198 us

profile of v2, /device:TPU:6, one launch (start us, length us, event | category | flops | bytes accessed | tf_op | source)
XLA Modules:
  0.0 199.7 jit_solution(8536375957379669341)
XLA Ops:
  0.0 0.0 copy-start.1
  0.0 0.7 copy-done.1
  0.7 0.0 copy-start
  0.7 0.7 copy-done
  1.3 197.5 %shard_map.55 = bf16[256,1024]{1,0:T(8,128)(2,1)S(1)} custom-call(s32[1,2]{1,0:T(1,128)S(1)} %copy-done.1, s32[1,4,16]{2,1,0:T(4,128)S(1)} %bitcast.3, bf16[1,256,1024]{2,1,0:T(8,128)(2,1)} %q_hbm.1, bf16[1,256,1024]{2,1,0:T(8,128)(2,1)} %k_hbm.1, bf16[1,256,1024]{2,1,0:T(8,128)(2,1)} %v_hbm.1), custom_call_target="tpu_custom_call" | custom-call | tf_op jit(solution)/shard_map/pallas_call | solution.py:471
  198.9 0.8 copy.7
Async XLA Ops:
  0.0 0.7 copy-start.1
  0.7 0.7 copy-start

commit v3 on v1

--- a/solution.py
+++ b/solution.py
@@ -14,7 +14,8 @@
 WINDOW = HP // 2
 UNITS = 16
 SPAN = 4
-ROWS = 144
+PIECE = 16
+PIECES = PAIR // PIECE
 
 big_negative = -1e30
 MESH = pl.DeviceIdType.MESH
@@ -37,8 +38,8 @@
 
 
 def kernel(
-    tissue_hbm, routes_hbm, q_hbm, k_hbm, v_hbm, out,
-    tissue, routes, q_rows, k_rows, v_rows, kv, tis, work_o, work_r, work_l, qs, tab, tabv, tabs, tabo, places,
+    small_hbm, q_hbm, k_hbm, v_hbm, out,
+    routes, q_rows, k_rows, v_rows, kv, tis, work_o, work_r, work_l, qs, tab, tabv, tabs, tabo, places,
     ret_out, ret_in, own_acc, own_stat,
     rs, rr, ls, lr, trs, trr, tls, tlr, q_send, q_recv, t_send, t_recv, ret_s, ret_r, loc,
 ):
@@ -49,8 +50,7 @@
         pltpu.make_async_copy(k_hbm.at[0], k_rows, loc.at[0]),
         pltpu.make_async_copy(v_hbm.at[0], v_rows, loc.at[1]),
         pltpu.make_async_copy(q_hbm.at[0], q_rows, loc.at[2]),
-        pltpu.make_async_copy(routes_hbm.at[0], routes, loc.at[5]),
-        pltpu.make_async_copy(tissue_hbm, tissue, loc.at[6]),
+        pltpu.make_async_copy(small_hbm.at[0], routes, loc.at[5]),
     ]
     for load in loads:
         load.start()
@@ -130,7 +130,7 @@
     for load in loads[3:]:
         load.wait()
     for t in range(2):
-        tis[0, t] = jnp.full((8, 128), (tissue[0, t] == 1).astype(jnp.int32), jnp.int32)
+        tis[0, t] = jnp.full((8, 128), (routes[SPAN, t] == 1).astype(jnp.int32), jnp.int32)
     tis_right(1).start()
     tis_left(1).start()
 
@@ -228,11 +228,14 @@
                 preferred_element_type=jnp.float32,
             )
             four = by_head(shift) + by_head(total)
-            done.append((job, fold(both), jnp.concatenate(four * 4, axis=0)))
+            done.append((job, fold(both), jnp.concatenate(four * 2, axis=0)))
             ready = later
-        for (work, d, dy, c), folded, stat in done:
-            ret_out[dy, d, c, 0:PAIR, :] = folded.astype(jnp.bfloat16)
-            ret_out[dy, d, c, PAIR:ROWS, :] = stat.astype(jnp.bfloat16)
+        for i, ((work, d, dy, c), folded, stat) in enumerate(done):
+            pieces = folded.astype(jnp.bfloat16).reshape(PIECES, PIECE, TILE)
+            ret_out[dy, d, c * PIECES : (c + 1) * PIECES] = pieces
+            if c == 1:
+                both = jnp.concatenate([done[i - 1][2], stat], axis=0)
+                ret_out[dy, d, 2 * PIECES] = both.astype(jnp.bfloat16)
 
     def ret_copy(dy, d):
         back = (NY - dy) % NY
@@ -397,7 +400,10 @@
     def combine(u):
         tile, g = u // HP, u % HP
         spots = [(places[2 * (u * SPAN + j)], places[2 * (u * SPAN + j) + 1]) for j in range(SPAN)]
-        stats = [ret_in[a, c, PAIR:ROWS, :].astype(jnp.float32) for a, c in spots]
+        stats = []
+        for a, c in spots:
+            both = ret_in[a, 2 * PIECES].astype(jnp.float32)
+            stats.append(jnp.where(c == 0, both[0:8], both[8:16]))
         own = own_stat[u]
         rows = []
         for h in range(2):
@@ -415,7 +421,9 @@
             inv = 1.0 / den
             num = own_acc[u, span, :] * (own_w * inv)
             for (a, c), w in zip(spots, ws):
-                num = num + ret_in[a, c, span, :].astype(jnp.float32) * (w * inv)
+                first = c * PIECES + h * (PIECES // 2)
+                part = jnp.concatenate([ret_in[a, first + i] for i in range(PIECES // 2)], axis=0)
+                num = num + part.astype(jnp.float32) * (w * inv)
             rows.append(num)
         result = jnp.concatenate(rows, axis=0)
         rows_at = pl.ds(pl.multiple_of(tile * TILE, TILE), TILE)
@@ -428,6 +436,8 @@
 
 
 def local(queries, key_rows, values, tissue, routes):
+    wide = jnp.pad(tissue[:, None], ((0, 0), (0, 0), (0, UNITS - tissue.shape[1])))
+    small = jnp.concatenate([routes.transpose(0, 2, 1), wide], axis=1)
     vmem = pl.BlockSpec(memory_space=pltpu.VMEM)
     hbm = pl.BlockSpec(memory_space=pltpu.HBM)
     dma = pltpu.SemaphoreType.DMA
@@ -437,11 +447,10 @@
     out = pl.pallas_call(
         kernel,
         out_shape=jax.ShapeDtypeStruct(rows, jnp.bfloat16),
-        in_specs=[hbm] * 5,
+        in_specs=[hbm] * 4,
         out_specs=vmem,
         scratch_shapes=[
-            pltpu.SMEM((1, 2), jnp.int32),
-            pltpu.SMEM((SPAN, UNITS), jnp.int32),
+            pltpu.SMEM((SPAN + 1, UNITS), jnp.int32),
             pltpu.VMEM(rows, jnp.bfloat16),
             pltpu.VMEM(rows, jnp.bfloat16),
             pltpu.VMEM(rows, jnp.bfloat16),
@@ -456,19 +465,19 @@
             pltpu.SMEM((NY, 8, 128), jnp.int32),
             pltpu.SMEM((NY, 8, 128), jnp.int32),
             pltpu.SMEM((2 * UNITS * SPAN,), jnp.int32),
-            pltpu.VMEM((NY, NZ, 2, ROWS, TILE), jnp.bfloat16),
-            pltpu.VMEM((NY * NZ, 2, ROWS, TILE), jnp.bfloat16),
+            pltpu.VMEM((NY, NZ, 2 * PIECES + 1, PIECE, TILE), jnp.bfloat16),
+            pltpu.VMEM((NY * NZ, 2 * PIECES + 1, PIECE, TILE), jnp.bfloat16),
             pltpu.VMEM((UNITS, PAIR, TILE), jnp.float32),
             pltpu.VMEM((UNITS, 8, 128), jnp.float32),
             dma((steps, HP)), dma((steps, HP)), dma((steps, HP)), dma((steps, HP)),
             dma((steps,)), dma((steps,)), dma((steps,)), dma((steps,)),
             dma((3, 2)), dma((3, 2)), dma((NY,)), dma((NY,)),
-            dma((NY, NZ)), dma((NY, NZ)), dma((7,)),
+            dma((NY, NZ)), dma((NY, NZ)), dma((6,)),
         ],
         compiler_params=pltpu.CompilerParams(
             collective_id=0, has_side_effects=True, vmem_limit_bytes=53 * 1024 * 1024
         ),
-    )(tissue, routes.transpose(0, 2, 1), queries, key_rows, values)
+    )(small, queries, key_rows, values)
     return out[None]
 
 

time: 199 us -> 198 us (level)
  no operation moved by 1% of the time
where the time goes in v3:
time: 198 us
  Pallas kernels  196 us (99%)
    pallas_call x1, Pallas kernels, local(): pl.pallas_call(kernel, out_shape=jax.ShapeDtypeStruct(rows, jnp.bfloat16)...  196 us

profile of v3, /device:TPU:6, one launch (start us, length us, event | category | flops | bytes accessed | tf_op | source)
XLA Modules:
  0.0 197.7 jit_solution(16237809749358045886)
XLA Ops:
  0.0 0.0 copy-start
  0.0 0.0 copy-start.1
  0.0 0.7 copy-done
  0.7 0.0 copy-done.1
  0.7 196.2 %shard_map.55 = bf16[256,1024]{1,0:T(8,128)(2,1)S(1)} custom-call(s32[1,5,16]{2,1,0:T(8,128)S(1)} %pad_add_fusion.small_hbm, bf16[1,256,1024]{2,1,0:T(8,128)(2,1)} %q_hbm.1, bf16[1,256,1024]{2,1,0:T(8,128)(2,1)} %k_hbm.1, bf16[1,256,1024]{2,1,0:T(8,128)(2,1)} %v_hbm.1), custom_call_target="tpu_custom_call" | custom-call | tf_op jit(solution)/shard_map/pallas_call | solution.py:447
  196.9 0.8 copy.7
  (1 shorter events, 0.0 us)
Async XLA Ops:
  0.0 0.7 copy-start
  0.0 0.7 copy-start.1

commit v4 on v3

--- a/solution.py
+++ b/solution.py
@@ -11,7 +11,8 @@
 HP = 8
 PAIR = 128
 HALF = NZ // 2
-WINDOW = HP // 2
+SPLIT = HP // 2
+AHEAD = 6
 UNITS = 16
 SPAN = 4
 PIECE = 16
@@ -77,7 +78,7 @@
         return remote(kv.at[s - 1, c], kv.at[s, c], rs.at[s, c], rr.at[s, c], right)
 
     def chunk_left(s, c):
-        pair = (c + WINDOW) % HP
+        pair = (c + SPLIT) % HP
         return remote(
             kv.at[(NZ + 1 - s) % NZ, pair], kv.at[NZ - s, pair], ls.at[s, c], lr.at[s, c], left
         )
@@ -119,13 +120,15 @@
 
     loads[0].wait()
     loads[1].wait()
-    for c in range(WINDOW):
-        lay_pair(c)
-        lay_pair(c + WINDOW)
+    for c in range(HP):
+        if c < SPLIT:
+            lay_pair(c)
+            lay_pair(c + SPLIT)
         if c == 0:
             pl.semaphore_wait(barrier, 2 + NY - 1)
-        chunk_right(1, c).start()
-        chunk_left(1, c).start()
+        if c < AHEAD:
+            chunk_right(1, c).start()
+            chunk_left(1, c).start()
 
     for load in loads[3:]:
         load.wait()
@@ -266,11 +269,15 @@
             work[g] = kv[d, g]
 
     def relay(s, c):
-        later, chunk = s + (c + WINDOW) // HP, (c + WINDOW) % HP
+        later, chunk = s + (c + AHEAD) // HP, (c + AHEAD) % HP
         chunk_right(s, c).wait_send()
-        chunk_right(later, chunk).start()
         chunk_left(s, c).wait_send()
-        chunk_left(later, chunk).start()
+
+        @pl.when((later < HALF) | (chunk < SPLIT))
+        def _():
+            chunk_right(later, chunk).start()
+            chunk_left(later, chunk).start()
+
         chunk_right(s, c).wait_recv()
         chunk_left(s, c).wait_recv()
 
@@ -361,10 +368,15 @@
             @pl.when(s < HALF)
             def _():
                 relay(s, 2 * dy)
+
+            slots([(work_r, before_r, dy, c) for c in range(2)])
+            give_back(dy, before_r)
+
+            @pl.when(s < HALF)
+            def _():
                 relay(s, 2 * dy + 1)
 
-            slots([(work, d, dy, c) for work, d in ((work_r, before_r), (work_l, before_l)) for c in range(2)])
-            give_back(dy, before_r)
+            slots([(work_l, before_l, dy, c) for c in range(2)])
             give_back(dy, before_l)
 
             @pl.when(s == 2)
@@ -377,11 +389,11 @@
     for d in (HALF - 2, HALF + 2, HALF - 1, HALF + 1):
         ret_wait(d)
 
-    for c in range(WINDOW):
+    for c in range(SPLIT):
         chunk_right(HALF, c).wait_recv()
         work_r[c] = kv[HALF, c]
         chunk_left(HALF, c).wait_recv()
-        work_r[c + WINDOW] = kv[HALF, c + WINDOW]
+        work_r[c + SPLIT] = kv[HALF, c + SPLIT]
 
     @pl.loop(0, NY // 2)
     def _(i):
@@ -390,7 +402,7 @@
         for dy in pair:
             give_back(dy, HALF)
 
-    for c in range(WINDOW):
+    for c in range(SPLIT):
         chunk_right(HALF, c).wait_send()
         chunk_left(HALF, c).wait_send()
     ret_wait(HALF)

time: 198 us -> 198 us (level)
  no operation moved by 1% of the time
where the time goes in v4:
time: 198 us; the launch traced here: 197 us
  Pallas kernels  196 us (99%)
    pallas_call x1, Pallas kernels, local(): pl.pallas_call(kernel, out_shape=jax.ShapeDtypeStruct(rows, jnp.bfloat16)...  196 us

profile of v4, /device:TPU:6, one launch (start us, length us, event | category | flops | bytes accessed | tf_op | source)
XLA Modules:
  0.0 197.4 jit_solution(9135781938197729608)
XLA Ops:
  0.0 0.0 copy-start
  0.0 0.0 copy-start.1
  0.0 0.7 copy-done
  0.7 0.0 copy-done.1
  0.7 195.9 %shard_map.55 = bf16[256,1024]{1,0:T(8,128)(2,1)S(1)} custom-call(s32[1,5,16]{2,1,0:T(8,128)S(1)} %pad_add_fusion.small_hbm, bf16[1,256,1024]{2,1,0:T(8,128)(2,1)} %q_hbm.1, bf16[1,256,1024]{2,1,0:T(8,128)(2,1)} %k_hbm.1, bf16[1,256,1024]{2,1,0:T(8,128)(2,1)} %v_hbm.1), custom_call_target="tpu_custom_call" | custom-call | tf_op jit(solution)/shard_map/pallas_call | solution.py:459
  196.6 0.8 copy.7
  (1 shorter events, 0.0 us)
Async XLA Ops:
  0.0 0.7 copy-start
  0.0 0.7 copy-start.1

commit v5 on v4

--- a/solution.py
+++ b/solution.py
@@ -12,7 +12,7 @@
 PAIR = 128
 HALF = NZ // 2
 SPLIT = HP // 2
-AHEAD = 6
+AHEAD = 7
 UNITS = 16
 SPAN = 4
 PIECE = 16
@@ -379,7 +379,7 @@
             slots([(work_l, before_l, dy, c) for c in range(2)])
             give_back(dy, before_l)
 
-            @pl.when(s == 2)
+            @pl.when(s == 3)
             def _():
                 slots([(work_o, 0, dy, c) for c in range(2)])
                 give_back(dy, 0)

time: 198 us -> 198 us (level)
  no operation moved by 1% of the time
where the time goes in v5:
time: 198 us; the launch traced here: 197 us
  Pallas kernels  196 us (99%)
    pallas_call x1, Pallas kernels, local(): pl.pallas_call(kernel, out_shape=jax.ShapeDtypeStruct(rows, jnp.bfloat16)...  196 us

profile of v5, /device:TPU:6, one launch (start us, length us, event | category | flops | bytes accessed | tf_op | source)
XLA Modules:
  0.0 197.4 jit_solution(4120280615839214474)
XLA Ops:
  0.0 0.0 copy-start
  0.0 0.0 copy-start.1
  0.0 0.7 copy-done
  0.7 0.0 copy-done.1
  0.7 195.9 %shard_map.55 = bf16[256,1024]{1,0:T(8,128)(2,1)S(1)} custom-call(s32[1,5,16]{2,1,0:T(8,128)S(1)} %pad_add_fusion.small_hbm, bf16[1,256,1024]{2,1,0:T(8,128)(2,1)} %q_hbm.1, bf16[1,256,1024]{2,1,0:T(8,128)(2,1)} %k_hbm.1, bf16[1,256,1024]{2,1,0:T(8,128)(2,1)} %v_hbm.1), custom_call_target="tpu_custom_call" | custom-call | tf_op jit(solution)/shard_map/pallas_call | solution.py:459
  196.6 0.8 copy.7
  (1 shorter events, 0.0 us)
Async XLA Ops:
  0.0 0.7 copy-start
  0.0 0.7 copy-start.1

commit v6 on v4

--- a/solution.py
+++ b/solution.py
@@ -441,10 +441,10 @@
         rows_at = pl.ds(pl.multiple_of(tile * TILE, TILE), TILE)
         out[rows_at, pl.ds(pl.multiple_of(g * PAIR, PAIR), PAIR)] = result.T.astype(jnp.bfloat16)
 
-    @pl.loop(0, UNITS // 4)
+    @pl.loop(0, UNITS // 8)
     def _(i):
-        for k in range(4):
-            combine(4 * i + k)
+        for k in range(8):
+            combine(8 * i + k)
 
 
 def local(queries, key_rows, values, tissue, routes):

time: 198 us -> 197 us (level)
  no operation moved by 1% of the time
where the time goes in v6:
time: 197 us
  Pallas kernels  196 us (99%)
    pallas_call x1, Pallas kernels, local(): pl.pallas_call(kernel, out_shape=jax.ShapeDtypeStruct(rows, jnp.bfloat16)...  196 us

profile of v6, /device:TPU:6, one launch (start us, length us, event | category | flops | bytes accessed | tf_op | source)
XLA Modules:
  0.0 197.2 jit_solution(17479645148551908025)
XLA Ops:
  0.0 0.0 copy-start
  0.0 0.0 copy-start.1
  0.0 0.7 copy-done
  0.7 0.0 copy-done.1
  0.7 195.7 %shard_map.55 = bf16[256,1024]{1,0:T(8,128)(2,1)S(1)} custom-call(s32[1,5,16]{2,1,0:T(8,128)S(1)} %pad_add_fusion.small_hbm, bf16[1,256,1024]{2,1,0:T(8,128)(2,1)} %q_hbm.1, bf16[1,256,1024]{2,1,0:T(8,128)(2,1)} %k_hbm.1, bf16[1,256,1024]{2,1,0:T(8,128)(2,1)} %v_hbm.1), custom_call_target="tpu_custom_call" | custom-call | tf_op jit(solution)/shard_map/pallas_call | solution.py:459
  196.4 0.8 copy.7
  (1 shorter events, 0.0 us)
Async XLA Ops:
  0.0 0.7 copy-start
  0.0 0.7 copy-start.1
